TPU v7x, 512 devices: a whole 4x4x16 slice. The times are simulated.
512 devices in a mesh: dp: 32 (over z, core), fsdp: 16 (over x, y).
Axes of the slice: x: 4, y: 4, z: 16, core: 2. Of those that a mesh axis runs over, the one named last changes fastest.
Arguments:
- token_ids: int32 [65536], P(('dp', 'fsdp')), may hold values from 0 to 50431, as said below
- activations: bfloat16 [65536, 3072], P(('dp', 'fsdp'))
- grad_out: bfloat16 [65536, 3072], P(('dp', 'fsdp')), may hold values from -0.13183594 to 0.13183594
- error_buffer: bfloat16 [32, 3072, 3072], P('dp', 'fsdp'), may hold values from -6 to 6
- init_q: float32 [3072, 8], replicated, may hold values from -6 to 6
Outputs:
- p_factor: float32 [3072, 8], P('fsdp')
- q_factor: float32 [3072, 8], replicated
- error_next: bfloat16 [32, 3072, 3072], P('dp', 'fsdp')
Inputs may be any that keep to these rules, and one draw needn't show every extreme that they name: `token_ids`: id 1 is padding; on the rows of each device it forms a tail (possibly empty), and each device's first row holds id 0.
All inputs are finite; a program needn't handle non-finite values.
Results may differ from a plain program's by a relative error of at most 0.0006.
Values may be sent and summed in bfloat16 or wider, within the bound.
No kernel may reach another device: no remote copies, remote signals or barrier semaphores. Data moves between devices by JAX's collectives and lax.ppermute only.
A program may use at most 64 MiB of HBM per device.

v0:
```python
import jax
import jax.numpy as jnp
from jax import lax
from jax.sharding import PartitionSpec as P


def orthonormal_columns(p_rows):
    highest = lax.Precision.HIGHEST
    finished = []
    for index_col in range(p_rows.shape[1]):
        column = p_rows[:, index_col]
        if finished:
            stacked = jnp.stack(finished, axis=1)
            inner_vals = lax.psum(jnp.dot(column, stacked, precision=highest), "fsdp")
            column = column - jnp.dot(stacked, inner_vals, precision=highest)
        norm_square = lax.psum(jnp.sum(column * column), "fsdp")
        finished.append(column / jnp.sqrt(norm_square))
    return jnp.stack(finished, axis=1)


def on_device(token_ids, activations, grad_out, error_buffer, init_q):
    highest = lax.Precision.HIGHEST
    replicas = lax.axis_size("dp")
    valid_rows = (token_ids != 1).astype(grad_out.dtype)
    masked_grad = grad_out * valid_rows[:, None]
    x_cols = lax.all_to_all(activations, "fsdp", split_axis=1, concat_axis=0, tiled=True)
    error_rows = error_buffer[0]
    grad_rows = lax.dot_general(
        x_cols,
        lax.all_gather(masked_grad, "fsdp", axis=0, tiled=True),
        (((0,), (0,)), ((), ())),
        preferred_element_type=jnp.float32,
    )
    merged = grad_rows + error_rows.astype(jnp.float32)
    p_local = jnp.dot(merged, init_q, precision=highest)
    p_mean = lax.psum(p_local, "dp") / replicas
    ortho_basis = orthonormal_columns(p_mean)
    q_local = jnp.einsum(
        "rd,rk->dk", merged, ortho_basis, precision=highest, preferred_element_type=jnp.float32
    )
    q_factor = lax.psum(q_local, ("dp", "fsdp")) / replicas
    error_next = (merged - jnp.dot(ortho_basis, q_factor.T, precision=highest)).astype(jnp.bfloat16)
    return (ortho_basis, q_factor, error_next[None])


def solution(mesh):
    return jax.shard_map(
        on_device,
        mesh=mesh,
        in_specs=(
            P(("dp", "fsdp")),
            P(("dp", "fsdp"), None),
            P(("dp", "fsdp"), None),
            P("dp", "fsdp", None),
            P(),
        ),
        out_specs=(P("fsdp", None), P(), P("dp", "fsdp", None)),
        check_vma=False,
    )
```

profile of v0, /device:TPU:1, one launch (start us, length us, event | category | flops | bytes accessed | tf_op | source)
XLA Modules:
  0.0 1197.7 jit_solution(5980001329945168853)
XLA Ops:
  8.0 2.1 broadcast_multiply_fusion
  10.6 19.1 %all_to_all.19 = bf16[128,16,192]{0,2,1:T(8,128)(2,1)S(1)} all-to-all(bf16[128,16,192]{0,2,1:T(8,128)(2,1)S(1)} %bitcast.83), channel_id=1, replica_groups=mesh['dp'=32,'fsdp'=16] {'fsdp'}, dimensions={1} | all-to-all | bytes 1572864 | tf_op jit(solution)/shard_map/all_to_all | solution.py:26
  29.7 92.6 %all-gather.2.cloned.1.call-done = bf16[2048,3072]{1,0:T(8,128)(2,1)} async-done(((bf16[128,3072]{1,0:T(8,128)(2,1)}), bf16[2048,3072]{1,0:T(8,128)(2,1)}) %all-gather.2.cloned.1.call-update) | async-done | bytes 12582928 | tf_op jit(solution)/shard_map/all_gather | solution.py:30
  122.3 7.6 fusion
  130.0 1.9 fusion.29
  131.9 48.0 %psum.119 = f32[192,8]{0,1:T(8,128)S(1)} all-reduce(f32[192,8]{0,1:T(8,128)S(1)} %fusion.29), channel_id=1, replica_groups=mesh['dp'=32,'fsdp'=16] {'dp'}, use_global_device_ids=true, to_apply=%region_0.0 | all-reduce | flops 1536 | bytes 12288 | tf_op jit(solution)/shard_map/psum | solution.py:36
  180.5 31.8 %psum.120 = f32[]{:T(128)} all-reduce(f32[]{:T(128)} %multiply_reduce_fusion.8), channel_id=1, replica_groups=mesh['dp'=32,'fsdp'=16] {'fsdp'}, use_global_device_ids=true, to_apply=%region_2.0 | all-reduce | flops 1 | bytes 8 | tf_op jit(solution)/shard_map/psum | solution.py:16
  213.6 29.1 %psum.121 = f32[]{:T(128)} all-reduce(f32[]{:T(128)} %multiply_reduce_fusion), channel_id=1, replica_groups=mesh['dp'=32,'fsdp'=16] {'fsdp'}, use_global_device_ids=true, to_apply=%region_3.0 | all-reduce | flops 1 | bytes 8 | tf_op jit(solution)/shard_map/psum | solution.py:14
  244.0 30.6 %psum.122 = f32[]{:T(128)} all-reduce(f32[]{:T(128)} %multiply_reduce_fusion.7), channel_id=1, replica_groups=mesh['dp'=32,'fsdp'=16] {'fsdp'}, use_global_device_ids=true, to_apply=%region_5.0 | all-reduce | flops 1 | bytes 8 | tf_op jit(solution)/shard_map/psum | solution.py:16
  276.1 29.1 %psum.123 = f32[2]{0:T(128)S(1)} all-reduce(f32[2]{0:T(128)S(1)} %convolution_bitcast_fusion.6), channel_id=1, replica_groups=mesh['dp'=32,'fsdp'=16] {'fsdp'}, use_global_device_ids=true, to_apply=%region_6.0 | all-reduce | flops 2 | bytes 16 | tf_op jit(solution)/shard_map/psum | solution.py:14
  305.9 30.0 %psum.124 = f32[]{:T(128)} all-reduce(f32[]{:T(128)} %get-tuple-element.13), channel_id=1, replica_groups=mesh['dp'=32,'fsdp'=16] {'fsdp'}, use_global_device_ids=true, to_apply=%region_8.0 | all-reduce | flops 1 | bytes 8 | tf_op jit(solution)/shard_map/psum | solution.py:16
  336.7 29.1 %psum.125 = f32[3]{0:T(128)S(1)} all-reduce(f32[3]{0:T(128)S(1)} %convolution_bitcast_fusion.5), channel_id=1, replica_groups=mesh['dp'=32,'fsdp'=16] {'fsdp'}, use_global_device_ids=true, to_apply=%region_9.0 | all-reduce | flops 3 | bytes 24 | tf_op jit(solution)/shard_map/psum | solution.py:14
  366.5 30.0 %psum.126 = f32[]{:T(128)} all-reduce(f32[]{:T(128)} %get-tuple-element.11), channel_id=1, replica_groups=mesh['dp'=32,'fsdp'=16] {'fsdp'}, use_global_device_ids=true, to_apply=%region_11.0 | all-reduce | flops 1 | bytes 8 | tf_op jit(solution)/shard_map/psum | solution.py:16
  397.3 29.5 %psum.127 = f32[4]{0:T(128)S(1)} all-reduce(f32[4]{0:T(128)S(1)} %convolution_bitcast_fusion.4), channel_id=1, replica_groups=mesh['dp'=32,'fsdp'=16] {'fsdp'}, use_global_device_ids=true, to_apply=%region_12.0 | all-reduce | flops 4 | bytes 32 | tf_op jit(solution)/shard_map/psum | solution.py:14
  427.6 29.6 %psum.128 = f32[]{:T(128)} all-reduce(f32[]{:T(128)} %get-tuple-element.9), channel_id=1, replica_groups=mesh['dp'=32,'fsdp'=16] {'fsdp'}, use_global_device_ids=true, to_apply=%region_14.0 | all-reduce | flops 1 | bytes 8 | tf_op jit(solution)/shard_map/psum | solution.py:16
  458.0 29.8 %psum.129 = f32[5]{0:T(128)S(1)} all-reduce(f32[5]{0:T(128)S(1)} %convolution_bitcast_fusion.3), channel_id=1, replica_groups=mesh['dp'=32,'fsdp'=16] {'fsdp'}, use_global_device_ids=true, to_apply=%region_15.0 | all-reduce | flops 5 | bytes 40 | tf_op jit(solution)/shard_map/psum | solution.py:14
  488.5 29.3 %psum.130 = f32[]{:T(128)} all-reduce(f32[]{:T(128)} %get-tuple-element.7), channel_id=1, replica_groups=mesh['dp'=32,'fsdp'=16] {'fsdp'}, use_global_device_ids=true, to_apply=%region_17.0 | all-reduce | flops 1 | bytes 8 | tf_op jit(solution)/shard_map/psum | solution.py:16
  518.7 30.6 %psum.131 = f32[6]{0:T(128)S(1)} all-reduce(f32[6]{0:T(128)S(1)} %convolution_bitcast_fusion.2), channel_id=1, replica_groups=mesh['dp'=32,'fsdp'=16] {'fsdp'}, use_global_device_ids=true, to_apply=%region_18.0 | all-reduce | flops 6 | bytes 48 | tf_op jit(solution)/shard_map/psum | solution.py:14
  550.0 29.3 %psum.132 = f32[]{:T(128)} all-reduce(f32[]{:T(128)} %get-tuple-element.5), channel_id=1, replica_groups=mesh['dp'=32,'fsdp'=16] {'fsdp'}, use_global_device_ids=true, to_apply=%region_20.0 | all-reduce | flops 1 | bytes 8 | tf_op jit(solution)/shard_map/psum | solution.py:16
  580.2 30.5 %psum.133 = f32[7]{0:T(128)S(1)} all-reduce(f32[7]{0:T(128)S(1)} %convolution_bitcast_fusion.1), channel_id=1, replica_groups=mesh['dp'=32,'fsdp'=16] {'fsdp'}, use_global_device_ids=true, to_apply=%region_21.0 | all-reduce | flops 7 | bytes 56 | tf_op jit(solution)/shard_map/psum | solution.py:14
  611.5 29.1 %psum.134 = f32[]{:T(128)} all-reduce(f32[]{:T(128)} %get-tuple-element.3), channel_id=1, replica_groups=mesh['dp'=32,'fsdp'=16] {'fsdp'}, use_global_device_ids=true, to_apply=%region_23.0 | all-reduce | flops 1 | bytes 8 | tf_op jit(solution)/shard_map/psum | solution.py:16
  641.3 2.0 fusion.30
  643.3 543.5 %all-reduce.2.cloned.1.call-done = f32[3072,8]{0,1:T(8,128)} async-done(((f32[3072,8]{0,1:T(8,128)}), f32[3072,8]{0,1:T(8,128)}) %all-reduce.2.cloned.1.call-update) | async-done | bytes 98320 | tf_op jit(solution)/shard_map/psum | solution.py:41
  1187.8 3.1 fusion.2
  (49 shorter events, 10.7 us)
Async XLA Ops:
  7.2 122.8 %copy-start = (f32[3072,8]{0,1:T(8,128)S(1)}, f32[3072,8]{0,1:T(8,128)}, u32[]{:S(2)}) copy-start(f32[3072,8]{0,1:T(8,128)} %param.9) | copy-start | bytes 294916
  7.2 3.0 copy-start.1
  7.2 115.1 %all-gather.2.cloned.1.call-start = ((), (), s32[]{:S(2)}) async-start(), calls=%async_computation.1 | async-start | bytes 13369344 | tf_op jit(solution)/shard_map/all_gather | solution.py:30
  10.1 1176.7 %all-reduce.2.cloned.1.call-start = ((), (), s32[]{:S(2)}) async-start(), calls=%async_computation.2 | async-start | bytes 196608 | tf_op jit(solution)/shard_map/psum | solution.py:41
  641.3 549.5 %copy-start.3 = (f32[192,8]{0,1:T(8,128)}, f32[192,8]{0,1:T(8,128)S(1)}, u32[]{:S(2)}) copy-start(f32[192,8]{0,1:T(8,128)S(1)} %stack.41) | copy-start | bytes 18436
  1187.8 3.1 copy-start.2
Sparse Core Ops, SparseCore 0:
  11.7 110.6 all-gather.1
  643.4 543.3 all-reduce.1
where the time goes:
time: 1200 us
  waiting for transfers between devices  636 us (53%)
  blocking collectives  514 us (43%)
  between operations  19.7 us (2%)
  matrix products  16.2 us (1%)
    psum x1, waiting for transfers between devices, on_device(): q_factor = lax.psum(q_local, ('dp', 'fsdp')) / replicas  544 us
    psum x8, blocking collectives, orthonormal_columns(): norm_square = lax.psum(jnp.sum(column * column), 'fsdp')  240 us
    psum x7, blocking collectives, orthonormal_columns(): inner_vals = lax.psum(jnp.dot(column, stacked, precision=highest), 'fsdp')  208 us
    all_gather x1, waiting for transfers between devices, on_device(): lax.all_gather(masked_grad, 'fsdp', axis=0, tiled=True)  92.6 us
    psum x1, blocking collectives, on_device(): p_mean = lax.psum(p_local, 'dp') / replicas  48 us
  transfers between devices with their start and end apart: 2, of which 2 were waited for; matrix products, arithmetic and copies ran while one was open for 0% of the time, Pallas kernels for 0%

commit v1 on v0

--- a/solution.py
+++ b/solution.py
@@ -11,7 +11,9 @@
         column = p_rows[:, index_col]
         if finished:
             stacked = jnp.stack(finished, axis=1)
-            inner_vals = lax.psum(jnp.dot(column, stacked, precision=highest), "fsdp")
+            inner_vals = jnp.sum(
+                lax.all_gather(jnp.dot(column, stacked, precision=highest), "fsdp"), axis=0
+            )
             column = column - jnp.dot(stacked, inner_vals, precision=highest)
         norm_square = lax.psum(jnp.sum(column * column), "fsdp")
         finished.append(column / jnp.sqrt(norm_square))

time: 1200 us -> 1200 us (level)
  blocking collectives: 514 us -> 495 us
    psum x7 -> x0, blocking collectives: 208 us -> none  [orthonormal_columns(): inner_vals = lax.psum(jnp.dot(column, stacked, precision=highest), 'fsdp')]
    unnamed x0 -> x7, blocking collectives: none -> 207 us
    all_to_all x1 -> x0, blocking collectives: 19.1 us -> none  [on_device(): lax.all_to_all(activations, 'fsdp', split_axis=1, concat_axis=0, tiled=True)]
  transfers between devices with their start and end apart: 2 -> 3, of which waited for: 2 -> 3; matrix products, arithmetic and copies ran while one was open for 0% -> 0% of each run, Pallas kernels for 0% -> 0%
where the time goes in v1:
time: 1200 us
  waiting for transfers between devices  644 us (54%)
  blocking collectives  495 us (41%)
  between operations  23.7 us (2%)
  matrix products  16 us (1%)
    psum x1, waiting for transfers between devices, on_device(): q_factor = lax.psum(q_local, ('dp', 'fsdp')) / replicas  543 us
    psum x8, blocking collectives, orthonormal_columns(): norm_square = lax.psum(jnp.sum(column * column), 'fsdp')  240 us
    unnamed x7, blocking collectives  207 us
    all_gather x1, waiting for transfers between devices, on_device(): lax.all_gather(masked_grad, 'fsdp', axis=0, tiled=True)  92.7 us
    psum x1, blocking collectives, on_device(): p_mean = lax.psum(p_local, 'dp') / replicas  48 us
  transfers between devices with their start and end apart: 3, of which 3 were waited for; matrix products, arithmetic and copies ran while one was open for 0% of the time, Pallas kernels for 0%

profile of v1, /device:TPU:1, one launch (start us, length us, event | category | flops | bytes accessed | tf_op | source)
XLA Modules:
  0.0 1202.9 jit_solution(4406290757717115242)
XLA Ops:
  8.0 2.1 broadcast_multiply_fusion
  11.3 7.6 all-to-all-start
  22.2 7.4 all-to-all-done
  29.6 92.7 %all-gather.8.cloned.1.call-done = bf16[2048,3072]{1,0:T(8,128)(2,1)} async-done(((bf16[128,3072]{1,0:T(8,128)(2,1)}), bf16[2048,3072]{1,0:T(8,128)(2,1)}) %all-gather.8.cloned.1.call-update) | async-done | bytes 12582928 | tf_op jit(solution)/shard_map/all_gather | solution.py:32
  122.3 7.5 fusion
  131.7 48.0 %psum.70 = f32[192,8]{0,1:T(8,128)S(1)} all-reduce(f32[192,8]{0,1:T(8,128)S(1)} %fusion.29), channel_id=1, replica_groups=mesh['dp'=32,'fsdp'=16] {'dp'}, use_global_device_ids=true, to_apply=%region_0.0 | all-reduce | flops 1536 | bytes 12288 | tf_op jit(solution)/shard_map/psum | solution.py:38
  181.0 31.8 %psum.71 = f32[]{:T(128)} all-reduce(f32[]{:T(128)} %multiply_reduce_fusion.8), channel_id=1, replica_groups=mesh['dp'=32,'fsdp'=16] {'fsdp'}, use_global_device_ids=true, to_apply=%region_2.0 | all-reduce | flops 1 | bytes 8 | tf_op jit(solution)/shard_map/psum | solution.py:18
  216.2 28.5 %all-reduce = f32[16]{0:T(128)S(1)} all-reduce(f32[16]{0:T(128)S(1)} %dynamic-update-slice), channel_id=1, replica_groups=mesh['dp'=32,'fsdp'=16] {'fsdp'}, use_global_device_ids=true, to_apply=%add | all-reduce | flops 16 | bytes 128
  247.2 30.6 %psum.72 = f32[]{:T(128)} all-reduce(f32[]{:T(128)} %multiply_reduce_fusion.7), channel_id=1, replica_groups=mesh['dp'=32,'fsdp'=16] {'fsdp'}, use_global_device_ids=true, to_apply=%region_5.0 | all-reduce | flops 1 | bytes 8 | tf_op jit(solution)/shard_map/psum | solution.py:18
  279.5 29.4 %all-reduce.1 = f32[32]{0:T(128)S(1)} all-reduce(f32[32]{0:T(128)S(1)} %dynamic-update-slice.1), channel_id=2, replica_groups=mesh['dp'=32,'fsdp'=16] {'fsdp'}, use_global_device_ids=true, to_apply=%add.1 | all-reduce | flops 32 | bytes 256
  309.8 29.9 %psum.73 = f32[]{:T(128)} all-reduce(f32[]{:T(128)} %get-tuple-element.13), channel_id=1, replica_groups=mesh['dp'=32,'fsdp'=16] {'fsdp'}, use_global_device_ids=true, to_apply=%region_8.0 | all-reduce | flops 1 | bytes 8 | tf_op jit(solution)/shard_map/psum | solution.py:18
  340.8 29.3 %all-reduce.2 = f32[48]{0:T(128)S(1)} all-reduce(f32[48]{0:T(128)S(1)} %dynamic-update-slice.2), channel_id=3, replica_groups=mesh['dp'=32,'fsdp'=16] {'fsdp'}, use_global_device_ids=true, to_apply=%add.2 | all-reduce | flops 48 | bytes 384
  371.0 30.0 %psum.74 = f32[]{:T(128)} all-reduce(f32[]{:T(128)} %get-tuple-element.11), channel_id=1, replica_groups=mesh['dp'=32,'fsdp'=16] {'fsdp'}, use_global_device_ids=true, to_apply=%region_11.0 | all-reduce | flops 1 | bytes 8 | tf_op jit(solution)/shard_map/psum | solution.py:18
  402.0 29.6 %all-reduce.3 = f32[64]{0:T(128)S(1)} all-reduce(f32[64]{0:T(128)S(1)} %dynamic-update-slice.3), channel_id=4, replica_groups=mesh['dp'=32,'fsdp'=16] {'fsdp'}, use_global_device_ids=true, to_apply=%add.3 | all-reduce | flops 64 | bytes 512
  432.5 29.4 %psum.75 = f32[]{:T(128)} all-reduce(f32[]{:T(128)} %get-tuple-element.9), channel_id=1, replica_groups=mesh['dp'=32,'fsdp'=16] {'fsdp'}, use_global_device_ids=true, to_apply=%region_14.0 | all-reduce | flops 1 | bytes 8 | tf_op jit(solution)/shard_map/psum | solution.py:18
  463.0 29.8 %all-reduce.4 = f32[80]{0:T(128)S(1)} all-reduce(f32[80]{0:T(128)S(1)} %dynamic-update-slice.4), channel_id=5, replica_groups=mesh['dp'=32,'fsdp'=16] {'fsdp'}, use_global_device_ids=true, to_apply=%add.4 | all-reduce | flops 80 | bytes 640
  493.7 29.2 %psum.76 = f32[]{:T(128)} all-reduce(f32[]{:T(128)} %get-tuple-element.7), channel_id=1, replica_groups=mesh['dp'=32,'fsdp'=16] {'fsdp'}, use_global_device_ids=true, to_apply=%region_17.0 | all-reduce | flops 1 | bytes 8 | tf_op jit(solution)/shard_map/psum | solution.py:18
  524.0 30.5 %all-reduce.5 = f32[96]{0:T(128)S(1)} all-reduce(f32[96]{0:T(128)S(1)} %dynamic-update-slice.5), channel_id=6, replica_groups=mesh['dp'=32,'fsdp'=16] {'fsdp'}, use_global_device_ids=true, to_apply=%add.5 | all-reduce | flops 96 | bytes 768
  555.4 29.4 %psum.77 = f32[]{:T(128)} all-reduce(f32[]{:T(128)} %get-tuple-element.5), channel_id=1, replica_groups=mesh['dp'=32,'fsdp'=16] {'fsdp'}, use_global_device_ids=true, to_apply=%region_20.0 | all-reduce | flops 1 | bytes 8 | tf_op jit(solution)/shard_map/psum | solution.py:18
  585.9 29.8 %all-reduce.6 = f32[112]{0:T(128)S(1)} all-reduce(f32[112]{0:T(128)S(1)} %dynamic-update-slice.6), channel_id=7, replica_groups=mesh['dp'=32,'fsdp'=16] {'fsdp'}, use_global_device_ids=true, to_apply=%add.6 | all-reduce | flops 112 | bytes 896
  616.6 29.2 %psum.78 = f32[]{:T(128)} all-reduce(f32[]{:T(128)} %get-tuple-element.3), channel_id=1, replica_groups=mesh['dp'=32,'fsdp'=16] {'fsdp'}, use_global_device_ids=true, to_apply=%region_23.0 | all-reduce | flops 1 | bytes 8 | tf_op jit(solution)/shard_map/psum | solution.py:18
  646.6 2.0 fusion.30
  648.6 543.5 %all-reduce.9.cloned.1.call-done = f32[3072,8]{0,1:T(8,128)} async-done(((f32[3072,8]{0,1:T(8,128)}), f32[3072,8]{0,1:T(8,128)}) %all-reduce.9.cloned.1.call-update) | async-done | bytes 98320 | tf_op jit(solution)/shard_map/psum | solution.py:43
  1192.9 3.1 fusion.2
  (78 shorter events, 18.7 us)
Async XLA Ops:
  7.2 122.6 %copy-start = (f32[3072,8]{0,1:T(8,128)S(1)}, f32[3072,8]{0,1:T(8,128)}, u32[]{:S(2)}) copy-start(f32[3072,8]{0,1:T(8,128)} %param.9) | copy-start | bytes 294916
  7.2 2.9 copy-start.1
  7.2 115.1 %all-gather.8.cloned.1.call-start = ((), (), s32[]{:S(2)}) async-start(), calls=%async_computation.1 | async-start | bytes 13369344 | tf_op jit(solution)/shard_map/all_gather | solution.py:32
  11.3 18.3 %all-to-all-start = ((bf16[128,16,192]{0,2,1:T(8,128)(2,1)}), bf16[128,16,192]{0,2,1:T(8,128)(2,1)S(1)}, u32[]{:S(2)}, u32[]{:S(2)}) async-start(bf16[128,16,192]{0,2,1:T(8,128)(2,1)} %bitcast), calls=%async_computation | async-start | bytes 1572864 | tf_op jit(solution)/shard_map/all_to_all | solution.py:28
  18.9 1173.1 %all-reduce.9.cloned.1.call-start = ((), (), s32[]{:S(2)}) async-start(), calls=%async_computation.2 | async-start | bytes 196608 | tf_op jit(solution)/shard_map/psum | solution.py:43
  646.6 549.5 %copy-start.3 = (f32[192,8]{0,1:T(8,128)}, f32[192,8]{0,1:T(8,128)S(1)}, u32[]{:S(2)}) copy-start(f32[192,8]{0,1:T(8,128)S(1)} %stack.41) | copy-start | bytes 18436
  1192.9 3.1 copy-start.2
Sparse Core Ops, SparseCore 0:
  11.7 110.6 all-gather.7
  648.7 543.3 all-reduce.8
